TPU v7x, 128 devices: a whole 4x4x4 slice. The times are simulated.
128 devices in a mesh: dp: 8 (over y, z_hi), seq: 16 (over z_lo, x, core).
Axes of the slice: x: 4, y: 4, z: 4 (z_hi: 2, z_lo: 2; z = z_hi * 2 + z_lo), core: 2. Of those that a mesh axis runs over, the one named last changes fastest.
Arguments:
- frames: bfloat16 [8, 256, 256, 1280], P('dp', 'seq'), may hold values from -6 to 6
- map_weight: bfloat16 [1280, 8], replicated, may hold values from -0.15625 to 0.15625
- qkv_weight: bfloat16 [1280, 3840], replicated, may hold values from -8 to 8, as said below
- cotangent: bfloat16 [8, 2048, 1280], P('dp', 'seq'), may hold values from -6 to 6
Outputs:
- grad_qkv_weight: float32 [1280, 3840], P(None, 'seq')
Inputs may be any that keep to these rules, and one draw needn't show every extreme that they name: qkv_weight has mean zero and entries of order 1280 ** -0.5 times at most 40.
All inputs are finite; a program needn't handle non-finite values.
Results may differ from a plain program's by a relative error of at most 0.019.
Values may be sent and summed in bfloat16 or wider, within the bound.
No kernel may reach another device: no remote copies, remote signals or barrier semaphores. Data moves between devices by JAX's collectives and lax.ppermute only.
A program may use at most 128 MiB of HBM per device.

v0:
```python
import math
import jax
import jax.numpy as jnp
from jax import lax
from jax.sharding import PartitionSpec as P

HEAD_DIM = 80


def as_sent(array):
    return jax.tree.map(lambda a: a.astype(jnp.bfloat16) if a.dtype == jnp.float32 else a, array)


def learn_tokens(frames, map_weight):
    frame_count = frames.shape[0]
    width_all = frames.shape[2]
    logits = jnp.dot(frames.reshape(-1, width_all), map_weight, preferred_element_type=jnp.float32)
    token_maps = (
        jax.nn.sigmoid(logits).astype(jnp.bfloat16).reshape(frame_count, frames.shape[1], -1)
    )
    pooled = jnp.einsum("fps,fpd->fsd", token_maps, frames, preferred_element_type=jnp.float32)
    pooled = pooled.reshape(-1, width_all)
    centred = pooled - jnp.mean(pooled, axis=-1, keepdims=True)
    variance = jnp.mean(centred * centred, axis=-1, keepdims=True)
    return (centred * lax.rsqrt(variance + 1e-06)).astype(jnp.bfloat16)


def one_head(query_rows, key_rows, value_rows, upstream):
    length = query_rows.shape[0]
    block_rows = math.gcd(length, 512)
    block_count = length // block_rows
    scaling = 1.0 / math.sqrt(HEAD_DIM)

    def advance(totals, position):
        key_total, value_total = totals
        query_block = lax.dynamic_slice_in_dim(query_rows, position * block_rows, block_rows, 0)
        grad_block = lax.dynamic_slice_in_dim(upstream, position * block_rows, block_rows, 0)
        scores = (
            jnp.einsum("qd,kd->qk", query_block, key_rows, preferred_element_type=jnp.float32)
            * scaling
        )
        shifted = jnp.exp(scores - jnp.max(scores, axis=-1, keepdims=True))
        attention = shifted / jnp.sum(shifted, axis=-1, keepdims=True)
        rounded = attention.astype(jnp.bfloat16)
        attended = jnp.dot(rounded, value_rows, preferred_element_type=jnp.float32)
        row_dot = jnp.sum(grad_block.astype(jnp.float32) * attended, axis=-1, keepdims=True)
        grad_attention = jnp.einsum(
            "qd,kd->qk", grad_block, value_rows, preferred_element_type=jnp.float32
        )
        grad_scores = (attention * (grad_attention - row_dot) * scaling).astype(jnp.bfloat16)
        grad_query = jnp.dot(grad_scores, key_rows, preferred_element_type=jnp.float32).astype(
            jnp.bfloat16
        )
        key_total = key_total + jnp.einsum(
            "qk,qd->kd", grad_scores, query_block, preferred_element_type=jnp.float32
        )
        value_total = value_total + jnp.einsum(
            "qk,qd->kd", rounded, grad_block, preferred_element_type=jnp.float32
        )
        return ((key_total, value_total), grad_query)

    empty_rows = jnp.zeros((length, HEAD_DIM), jnp.float32)
    totals, grad_query = lax.scan(advance, (empty_rows, empty_rows), jnp.arange(block_count))
    grad_query = grad_query.reshape(length, HEAD_DIM)
    return jnp.concatenate(
        [grad_query, totals[0].astype(jnp.bfloat16), totals[1].astype(jnp.bfloat16)], axis=1
    )


def heads_backward(projected, upstream):
    query_rows = projected[:, 0:HEAD_DIM]
    key_rows = projected[:, HEAD_DIM : 2 * HEAD_DIM]
    value_rows = projected[:, 2 * HEAD_DIM : 3 * HEAD_DIM]
    pieces = [one_head(query_rows, key_rows, value_rows, upstream)]
    return jnp.concatenate(pieces, axis=1)


def heads_items(operands):
    return jax.vmap(heads_backward)(operands[0], operands[1])


def body(frames, map_weight, qkv_weight, cotangent):
    normed = learn_tokens(frames[0], map_weight)
    projected = jnp.dot(normed, qkv_weight, preferred_element_type=jnp.float32).astype(jnp.bfloat16)
    grads_heads = heads_items(
        (
            lax.all_to_all(projected[None], "seq", split_axis=2, concat_axis=1, tiled=True),
            lax.all_to_all(cotangent, "seq", split_axis=2, concat_axis=1, tiled=True),
        )
    )
    grads = lax.all_to_all(
        as_sent(grads_heads), "seq", split_axis=1, concat_axis=2, tiled=True
    ).astype(grads_heads.dtype)
    partial_value = jnp.einsum("td,tc->dc", normed, grads[0], preferred_element_type=jnp.float32)
    shares = lax.psum_scatter(partial_value, "seq", scatter_dimension=1, tiled=True)
    grad_weight = lax.psum(shares, "dp")
    return grad_weight


def solution(mesh):
    placed = (P("dp", "seq", None, None), P(), P(), P("dp", "seq", None))
    return jax.shard_map(
        body, mesh=mesh, in_specs=placed, out_specs=P(None, "seq"), check_vma=False
    )
```

profile of v0, /device:TPU:0, one launch (start us, length us, event | category | flops | bytes accessed | tf_op | source)
XLA Modules:
  0.0 412.4 jit_solution(12583312983164715362)
XLA Ops:
  6.5 1.4 copy.31
  8.5 7.5 %reduce.9 = bf16[1280,128]{1,0:T(8,128)(2,1)S(1)} reduce(bf16[1280,1,128]{2,1,0:T(2,128)(2,1)S(1)} %bitcast.145, bf16[]{:T(256)} %broadcast.113), dimensions={1}, to_apply=%bitcast.76.reduce_sub_computation | reduce | bytes 655362
  16.0 0.8 reshape.172
  16.8 5.8 %all-to-all-start.1 = ((bf16[16,2,5120]{2,1,0:T(2,128)(2,1)}), bf16[16,2,5120]{2,1,0:T(2,128)(2,1)S(1)}, u32[]{:S(2)}, u32[]{:S(2)}) async-start(bf16[16,2,5120]{2,1,0:T(2,128)(2,1)} %reshape.172), calls=%async_computation.1 | async-start | bytes 655360 | tf_op jit(solution)/shard_map/all_to_all | solution.py:88
  22.7 6.9 %fusion.32 = bf16[4096,8]{0,1:T(8,128)(2,1)S(1)} fusion(bf16[4096,1280]{1,0:T(8,128)(2,1)} %bitcast.134, bf16[1280,8]{0,1:T(8,128)(2,1)S(1)} %copy-done), kind=kOutput, calls=%fused_computation.42 | convolution fusion | flops 84017152 | bytes 10571776 | tf_op jit(solution)/shard_map/dot_general | solution.py:17
  29.6 1.5 fusion.44
  31.6 6.3 %fusion.28 = bf16[1,128,3840]{2,1,0:T(8,128)(2,1)} fusion(bf16[1280,3840]{1,0:T(8,128)(2,1)} %param.8, f32[16,8,1280]{2,1,0:T(8,128)S(1)} %get-tuple-element.160, f32[128]{0:T(128)S(1)} %rsqrt.13, f32[128]{0:T(128)S(1)} %div.23), kind=kOutput, calls=%fused_computation.37 | convolution fusion | flops 1259274240 | bytes 11469824 | tf_op jit(solution)/shard_map/dot_general | solution.py:84
  37.9 3.7 copy.29
  41.5 22.0 %reduce.8 = bf16[3840,128]{1,0:T(8,128)(2,1)} reduce(bf16[3840,1,128]{2,1,0:T(2,128)(2,1)S(1)} %bitcast.137, bf16[]{:T(256)} %broadcast.113), dimensions={1}, to_apply=%bitcast.74.reduce_sub_computation | reduce | bytes 1966082
  63.5 3.1 reshape.170
  66.7 0.7 copy-done.3
  67.4 5.7 %all-to-all-start = ((bf16[16,2,15360]{2,1,0:T(2,128)(2,1)}), bf16[16,2,15360]{2,1,0:T(2,128)(2,1)S(1)}, u32[]{:S(2)}, u32[]{:S(2)}) async-start(bf16[16,2,15360]{2,1,0:T(2,128)(2,1)} %reshape.170), calls=%async_computation | async-start | bytes 1966080 | tf_op jit(solution)/shard_map/all_to_all | solution.py:87
  73.4 3.2 reshape.173
  76.7 1.1 copy.43
  77.9 11.0 %all-to-all-done = bf16[16,2,15360]{2,1,0:T(2,128)(2,1)S(1)} async-done(((bf16[16,2,15360]{2,1,0:T(2,128)(2,1)}), bf16[16,2,15360]{2,1,0:T(2,128)(2,1)S(1)}, u32[]{:S(2)}, u32[]{:S(2)}) %all-to-all-start) | async-done | bytes 983072 | tf_op jit(solution)/shard_map/all_to_all | solution.py:87
  88.9 3.2 reshape.171
  92.1 1.7 copy.42
  94.1 0.9 fusion.43
  95.3 1.2 copy.34
  96.5 42.3 %while.17 = (s32[]{:T(128)}, f32[1,2048,80]{1,2,0:T(8,128)S(1)}, f32[1,2048,80]{1,2,0:T(8,128)S(1)}, bf16[4,1,512,80]{2,3,1,0:T(8,128)(2,1)}, s32[4]{0:T(128)S(1...) while((s32[]{:T(128)}, f32[1,2048,80]{1,2,0:T(8,128)S(1)}, ...), condition=%wide.region_6.7_spmd.clone, body=%wide.region_2.6_spmd.clone.sunk | while | flops 1022130688 | bytes 40287472 | solution.py:63
  97.9 1.9 multiply_reduce_fusion.3
  99.7 0.8 fusion.78
  100.6 0.8 fusion.79
  101.4 0.8 fusion.80
  102.9 1.2 multiply_convert_fusion.3
  104.1 1.4 fusion.83
  105.6 1.5 fusion.81
  108.4 1.9 multiply_reduce_fusion.3
  110.3 0.8 fusion.78
  111.1 0.8 fusion.79
  112.0 0.8 fusion.80
  112.8 0.6 fusion.82
  113.4 1.3 multiply_convert_fusion.3
  114.7 1.4 fusion.83
  116.1 1.5 fusion.81
  119.0 1.9 multiply_reduce_fusion.3
  120.9 0.8 fusion.78
  121.7 0.8 fusion.79
  122.5 0.8 fusion.80
  123.4 0.6 fusion.82
  124.0 1.2 multiply_convert_fusion.3
  125.3 1.4 fusion.83
  126.7 1.5 fusion.81
  129.6 1.9 multiply_reduce_fusion.3
  131.4 0.8 fusion.78
  132.3 0.8 fusion.79
  133.1 0.8 fusion.80
  133.9 0.6 fusion.82
  134.6 1.3 multiply_convert_fusion.3
  135.8 1.4 fusion.83
  137.3 1.5 fusion.81
  138.8 1.0 copy.47
  139.9 1.0 pad_maximum_fusion
  140.9 4.6 %copy.37 = bf16[1,2048,240]{2,0,1:T(2,128)(2,1)S(1)} copy(bf16[1,2048,240]{1,2,0:T(8,128)(2,1)} %pad_maximum_fusion) | data formatting | bytes 1966080 | tf_op jit(solution)/shard_map/vmap()/concatenate | solution.py:65
  145.5 12.6 %reduce.10 = bf16[2048,240]{1,0:T(8,128)(2,1)} reduce(bf16[2048,1,240]{2,1,0:T(2,128)(2,1)S(1)} %bitcast.136, bf16[]{:T(256)} %broadcast.113), dimensions={1}, to_apply=%bitcast.78.reduce_sub_computation | reduce | bytes 1966082
  158.2 3.8 reshape.174
  161.9 19.1 %all_to_all.51 = bf16[16,2,15360]{2,1,0:T(2,128)(2,1)} all-to-all(bf16[16,2,15360]{2,1,0:T(2,128)(2,1)S(1)} %reshape.174), channel_id=1, replica_groups=mesh['dp'=8,'seq'=16] {'seq'}, dimensions={0} | all-to-all | bytes 1966080 | tf_op jit(solution)/shard_map/all_to_all | solution.py:91
  181.0 6.0 %reshape.175 = bf16[2048,1,240]{2,1,0:T(2,128)(2,1)S(1)} reshape(bf16[16,2,15360]{2,1,0:T(2,128)(2,1)} %all_to_all.51) | data formatting | bytes 1966080
  187.0 1.2 copy.44
  188.1 1.7 copy.40
  190.1 8.3 %fusion.36 = f32[1280,3840]{0,1:T(8,128)} fusion(bf16[128,3840]{0,1:T(8,128)(2,1)S(1)} %bitcast.140, f32[16,8,1280]{2,1,0:T(8,128)S(1)} %get-tuple-element.160, f32[16,8]{1,0:T(8,128)S(1)} %add_rsqrt_fusion, f32[16,8]{1,0:T(8,128)S(1)} %broadcast_multiply_fusion), kind=kOutput, calls=%fused_computation.51 | convolution fusion | flops 1258782720 | bytes 21300224 | tf_op jit(solution)/shard_map/td,tc->dc/dot_general | solution.py:94
  198.5 112.5 %reduce-scatter.2.cloned.1.call-done = f32[1280,240]{0,1:T(8,128)} async-done(((f32[1280,3840]{0,1:T(8,128)}), f32[1280,240]{0,1:T(8,128)}) %reduce-scatter.2.cloned.1.call-update) | async-done | bytes 1228816 | tf_op jit(solution)/shard_map/reduce_scatter | solution.py:95
  311.0 92.2 %all-reduce.2.cloned.1.call-done = f32[1280,240]{0,1:T(8,128)} async-done(((f32[1280,240]{0,1:T(8,128)}), f32[1280,240]{0,1:T(8,128)}) %all-reduce.2.cloned.1.call-update) | async-done | bytes 1228816 | tf_op jit(solution)/shard_map/psum | solution.py:96
  403.2 2.4 copy.66
  (37 shorter events, 5.6 us)
Async XLA Ops:
  6.5 16.1 %copy-start = (bf16[1280,8]{0,1:T(8,128)(2,1)S(1)}, bf16[1280,8]{0,1:T(8,128)(2,1)}, u32[]{:S(2)}) copy-start(bf16[1280,8]{0,1:T(8,128)(2,1)} %param.7) | copy-start | bytes 61444
  16.8 49.9 %all-to-all-start.1 = ((bf16[16,2,5120]{2,1,0:T(2,128)(2,1)}), bf16[16,2,5120]{2,1,0:T(2,128)(2,1)S(1)}, u32[]{:S(2)}, u32[]{:S(2)}) async-start(bf16[16,2,5120]{2,1,0:T(2,128)(2,1)} %reshape.172), calls=%async_computation.1 | async-start | bytes 655360 | tf_op jit(solution)/shard_map/all_to_all | solution.py:88
  22.7 7.0 %copy-start.2 = (bf16[1,16,256,1280]{3,2,1,0:T(8,128)(2,1)S(1)}, bf16[1,16,256,1280]{3,2,1,0:T(8,128)(2,1)}, u32[]{:S(2)}) copy-start(bf16[1,16,256,1280]{3,2,1,0:T(8,128)(2,1)} %param.6) | copy-start | bytes 31457284
  66.7 0.7 copy-start.3
  67.4 21.5 %all-to-all-start = ((bf16[16,2,15360]{2,1,0:T(2,128)(2,1)}), bf16[16,2,15360]{2,1,0:T(2,128)(2,1)S(1)}, u32[]{:S(2)}, u32[]{:S(2)}) async-start(bf16[16,2,15360]{2,1,0:T(2,128)(2,1)} %reshape.170), calls=%async_computation | async-start | bytes 1966080 | tf_op jit(solution)/shard_map/all_to_all | solution.py:87
  73.1 237.8 %reduce-scatter.2.cloned.1.call-start = ((), (), s32[]{:S(2)}) async-start(), calls=%async_computation.4 | async-start | bytes 20889600 | tf_op jit(solution)/shard_map/reduce_scatter | solution.py:95
  198.4 207.2 %copy-start.1 = (bf16[1280,8]{0,1:T(8,128)(2,1)S(1)}, bf16[1280,8]{0,1:T(8,128)(2,1)}, u32[]{:S(2)}) copy-start(bf16[1280,8]{0,1:T(8,128)(2,1)} %param.7) | copy-start | bytes 61444
  198.4 204.8 %all-reduce.2.cloned.1.call-start = ((), (), s32[]{:S(2)}) async-start(), calls=%async_computation.5 | async-start | bytes 2457600 | tf_op jit(solution)/shard_map/psum | solution.py:96
Sparse Core Ops, SparseCore 0:
  198.5 112.3 reduce-scatter.1
  313.6 89.5 all-reduce.1
where the time goes:
time: 414 us; the launch traced here: 412 us
  waiting for transfers between devices  216 us (52%)
  matrix products  53.1 us (13%)
  other arithmetic  50.4 us (12%)
  local copies, waits for them, and re-layouts  45.7 us (11%)
  blocking collectives  19.1 us (5%)
  between operations  13.6 us (3%)
  starting transfers between devices  11.9 us (3%)
    reduce_scatter x1, waiting for transfers between devices, body(): lax.psum_scatter(partial_value, 'seq', scatter_dimension=1, tiled=True)  112 us
    psum x1, waiting for transfers between devices, body(): grad_weight = lax.psum(shares, 'dp')  92.2 us
    unnamed x5, other arithmetic  42.1 us
    unnamed x22, local copies, waits for them, and re-layouts  30.7 us
    all_to_all x1, blocking collectives, body(): lax.all_to_all(as_sent(grads_heads), 'seq', split_axis=1, concat_axis=2,...  19.1 us
    all_to_all x1, waiting for transfers between devices, body(): lax.all_to_all(projected[None], 'seq', split_axis=2, concat_axis=1, tiled...  11 us
  transfers between devices with their start and end apart: 4, of which 3 were waited for; matrix products, arithmetic and copies ran while one was open for 12% of the time, Pallas kernels for 0%

commit v1 on v0

--- a/solution.py
+++ b/solution.py
@@ -84,7 +84,12 @@
     projected = jnp.dot(normed, qkv_weight, preferred_element_type=jnp.float32).astype(jnp.bfloat16)
     grads_heads = heads_items(
         (
-            lax.all_to_all(projected[None], "seq", split_axis=2, concat_axis=1, tiled=True),
+            jnp.concatenate(
+                lax.all_to_all(
+                    jnp.stack(jnp.split(projected[None], lax.axis_size("seq"), axis=2)), "seq", 0, 0
+                ),
+                axis=1,
+            ),
             lax.all_to_all(cotangent, "seq", split_axis=2, concat_axis=1, tiled=True),
         )
     )

time: 414 us -> 380 us (0.918)
  other arithmetic: 50.4 us -> 28.4 us
  local copies, waits for them, and re-layouts: 45.7 us -> 33.4 us
    unnamed x5 -> x4, other arithmetic: 42.1 us -> 20.1 us
    unnamed x22 -> x32, local copies, waits for them, and re-layouts: 30.7 us -> 20.8 us
  transfers between devices with their start and end apart: 4 -> 4, of which waited for: 3 -> 3; matrix products, arithmetic and copies ran while one was open for 12% -> 5% of each run, Pallas kernels for 0% -> 0%
where the time goes in v1:
time: 380 us; the launch traced here: 379 us
  waiting for transfers between devices  218 us (57%)
  matrix products  51.7 us (14%)
  local copies, waits for them, and re-layouts  33.4 us (9%)
  other arithmetic  28.4 us (7%)
  blocking collectives  19.1 us (5%)
  between operations  13.7 us (4%)
  starting transfers between devices  11.8 us (3%)
    reduce_scatter x1, waiting for transfers between devices, body(): lax.psum_scatter(partial_value, 'seq', scatter_dimension=1, tiled=True)  112 us
    psum x1, waiting for transfers between devices, body(): grad_weight = lax.psum(shares, 'dp')  92.2 us
    unnamed x32, local copies, waits for them, and re-layouts  20.8 us
    unnamed x4, other arithmetic  20.1 us
    all_to_all x1, blocking collectives, body(): lax.all_to_all(as_sent(grads_heads), 'seq', split_axis=1, concat_axis=2,...  19.1 us
    all_to_all x1, waiting for transfers between devices, body(): lax.all_to_all(jnp.stack(jnp.split(projected[None], lax.axis_size('seq'),...  13.3 us
    dot_general x1, matrix products, body(): jnp.einsum('td,tc->dc', normed, grads[0], preferred_element_type=jnp.floa...  8.26 us
  transfers between devices with their start and end apart: 4, of which 3 were waited for; matrix products, arithmetic and copies ran while one was open for 5% of the time, Pallas kernels for 0%

profile of v1, /device:TPU:0, one launch (start us, length us, event | category | flops | bytes accessed | tf_op | source)
XLA Modules:
  0.0 378.9 jit_solution(17876616027519644466)
XLA Ops:
  6.5 1.4 copy.20
  8.5 7.5 %reduce.8 = bf16[1280,128]{1,0:T(8,128)(2,1)S(1)} reduce(bf16[1280,1,128]{2,1,0:T(2,128)(2,1)S(1)} %bitcast.201, bf16[]{:T(256)} %broadcast.113), dimensions={1}, to_apply=%bitcast.135.reduce_sub_computation | reduce | bytes 655362
  16.0 0.8 reshape.174
  16.8 5.8 %all-to-all-start.1 = ((bf16[16,2,5120]{2,1,0:T(2,128)(2,1)}), bf16[16,2,5120]{2,1,0:T(2,128)(2,1)S(1)}, u32[]{:S(2)}, u32[]{:S(2)}) async-start(bf16[16,2,5120]{2,1,0:T(2,128)(2,1)} %reshape.174), calls=%async_computation.1 | async-start | bytes 655360 | tf_op jit(solution)/shard_map/all_to_all | solution.py:93
  22.6 6.9 %fusion.32 = bf16[4096,8]{0,1:T(8,128)(2,1)S(1)} fusion(bf16[4096,1280]{1,0:T(8,128)(2,1)} %bitcast.194, bf16[1280,8]{0,1:T(8,128)(2,1)S(1)} %copy-done), kind=kOutput, calls=%fused_computation.42 | convolution fusion | flops 84017152 | bytes 10571776 | tf_op jit(solution)/shard_map/dot_general | solution.py:17
  29.6 1.5 fusion.60
  31.6 5.3 %fusion.28 = bf16[1,128,3840]{2,1,0:T(8,128)(2,1)S(1)} fusion(bf16[1280,3840]{1,0:T(8,128)(2,1)} %param.8, f32[16,8,1280]{2,1,0:T(8,128)S(1)} %get-tuple-element.142, f32[128]{0:T(128)S(1)} %rsqrt.13, f32[128]{0:T(128)S(1)} %div.23), kind=kOutput, calls=%fused_computation.37 | convolution fusion | flops 1259274240 | bytes 11469824 | tf_op jit(solution)/shard_map/dot_general | solution.py:84
  38.2 1.3 copy.18
  39.5 5.7 %all-to-all-start = ((bf16[16,1,128,240]{2,3,1,0:T(8,128)(2,1)}), bf16[16,1,128,240]{2,3,1,0:T(8,128)(2,1)S(1)}, u32[]{:S(2)}, u32[]{:S(2)}) async-start(bf16[16,1,128,240]{2,3,1,0:T(8,128)(2,1)} %copy.18), calls=%async_computation | async-start | bytes 1966080 | tf_op jit(solution)/shard_map/all_to_all | solution.py:88
  45.5 1.0 reshape.175
  46.5 1.1 copy.31
  47.7 13.3 %all-to-all-done = bf16[16,1,128,240]{2,3,1,0:T(8,128)(2,1)S(1)} async-done(((bf16[16,1,128,240]{2,3,1,0:T(8,128)(2,1)}), bf16[16,1,128,240]{2,3,1,0:T(8,128)(2,1)S(1)}, u32[]{:S(2)}, u32[]{:S(2)}) %all-to-all-start) | async-done | bytes 983072 | tf_op jit(solution)/shard_map/all_to_all | solution.py:88
  61.1 0.9 fusion.59
  62.3 1.2 copy.23
  63.6 41.7 %while.17 = (s32[]{:T(128)}, f32[1,2048,80]{1,2,0:T(8,128)S(1)}, f32[1,2048,80]{1,2,0:T(8,128)S(1)}, bf16[4,1,512,80]{2,3,1,0:T(8,128)(2,1)}, s32[4]{0:T(128)S(1...) while((s32[]{:T(128)}, f32[1,2048,80]{1,2,0:T(8,128)S(1)}, ...), condition=%wide.region_6.7_spmd.clone, body=%wide.region_2.6_spmd.clone.sunk | while | flops 1022130688 | bytes 40287472 | solution.py:63
  63.6 0.6 dynamic_slice.6
  64.9 1.9 multiply_reduce_fusion.3
  66.8 0.8 fusion.95
  67.6 0.8 fusion.96
  68.4 0.8 fusion.97
  69.2 0.6 fusion.99
  69.9 1.1 multiply_convert_fusion.3
  71.0 1.4 fusion.100
  72.5 1.5 fusion.98
  74.0 0.6 dynamic_slice.6
  75.3 1.9 multiply_reduce_fusion.3
  77.2 0.8 fusion.95
  78.0 0.8 fusion.96
  78.9 0.8 fusion.97
  79.7 0.6 fusion.99
  80.3 1.1 multiply_convert_fusion.3
  81.5 1.4 fusion.100
  82.9 1.5 fusion.98
  84.5 0.6 dynamic_slice.6
  85.8 1.9 multiply_reduce_fusion.3
  87.6 0.8 fusion.95
  88.5 0.8 fusion.96
  89.3 0.8 fusion.97
  90.1 0.6 fusion.99
  90.8 1.1 multiply_convert_fusion.3
  91.9 1.4 fusion.100
  93.3 1.5 fusion.98
  94.9 0.6 dynamic_slice.6
  96.2 1.9 multiply_reduce_fusion.3
  98.1 0.8 fusion.95
  98.9 0.8 fusion.96
  99.7 0.8 fusion.97
  100.6 0.6 fusion.99
  101.2 1.1 multiply_convert_fusion.3
  102.3 1.4 fusion.100
  103.8 1.5 fusion.98
  105.3 1.0 copy.35
  106.4 1.0 pad_maximum_fusion
  107.4 4.6 %copy.26 = bf16[1,2048,240]{2,0,1:T(2,128)(2,1)S(1)} copy(bf16[1,2048,240]{1,2,0:T(8,128)(2,1)} %pad_maximum_fusion) | data formatting | bytes 1966080 | tf_op jit(solution)/shard_map/vmap()/concatenate | solution.py:65
  112.0 12.6 %reduce.9 = bf16[2048,240]{1,0:T(8,128)(2,1)} reduce(bf16[2048,1,240]{2,1,0:T(2,128)(2,1)S(1)} %bitcast.196, bf16[]{:T(256)} %broadcast.113), dimensions={1}, to_apply=%bitcast.137.reduce_sub_computation | reduce | bytes 1966082
  124.6 3.8 reshape.176
  128.4 19.1 %all_to_all.38 = bf16[16,2,15360]{2,1,0:T(2,128)(2,1)} all-to-all(bf16[16,2,15360]{2,1,0:T(2,128)(2,1)S(1)} %reshape.176), channel_id=1, replica_groups=mesh['dp'=8,'seq'=16] {'seq'}, dimensions={0} | all-to-all | bytes 1966080 | tf_op jit(solution)/shard_map/all_to_all | solution.py:96
  147.5 6.0 %reshape.177 = bf16[2048,1,240]{2,1,0:T(2,128)(2,1)S(1)} reshape(bf16[16,2,15360]{2,1,0:T(2,128)(2,1)} %all_to_all.38) | data formatting | bytes 1966080
  153.4 1.1 copy.32
  154.6 1.7 copy.29
  156.6 8.3 %fusion.36 = f32[1280,3840]{0,1:T(8,128)} fusion(bf16[128,3840]{0,1:T(8,128)(2,1)S(1)} %bitcast.198, f32[16,8,1280]{2,1,0:T(8,128)S(1)} %get-tuple-element.142, f32[16,8]{1,0:T(8,128)S(1)} %add_rsqrt_fusion, f32[16,8]{1,0:T(8,128)S(1)} %broadcast_multiply_fusion), kind=kOutput, calls=%fused_computation.51 | convolution fusion | flops 1258782720 | bytes 21300224 | tf_op jit(solution)/shard_map/td,tc->dc/dot_general | solution.py:99
  164.9 112.5 %reduce-scatter.2.cloned.1.call-done = f32[1280,240]{0,1:T(8,128)} async-done(((f32[1280,3840]{0,1:T(8,128)}), f32[1280,240]{0,1:T(8,128)}) %reduce-scatter.2.cloned.1.call-update) | async-done | bytes 1228816 | tf_op jit(solution)/shard_map/reduce_scatter | solution.py:100
  277.5 92.2 %all-reduce.2.cloned.1.call-done = f32[1280,240]{0,1:T(8,128)} async-done(((f32[1280,240]{0,1:T(8,128)}), f32[1280,240]{0,1:T(8,128)}) %all-reduce.2.cloned.1.call-update) | async-done | bytes 1228816 | tf_op jit(solution)/shard_map/psum | solution.py:101
  369.7 2.4 copy.68
  (47 shorter events, 3.6 us)
Async XLA Ops:
  6.5 16.1 %copy-start = (bf16[1280,8]{0,1:T(8,128)(2,1)S(1)}, bf16[1280,8]{0,1:T(8,128)(2,1)}, u32[]{:S(2)}) copy-start(bf16[1280,8]{0,1:T(8,128)(2,1)} %param.7) | copy-start | bytes 61444
  16.8 22.7 %all-to-all-start.1 = ((bf16[16,2,5120]{2,1,0:T(2,128)(2,1)}), bf16[16,2,5120]{2,1,0:T(2,128)(2,1)S(1)}, u32[]{:S(2)}, u32[]{:S(2)}) async-start(bf16[16,2,5120]{2,1,0:T(2,128)(2,1)} %reshape.174), calls=%async_computation.1 | async-start | bytes 655360 | tf_op jit(solution)/shard_map/all_to_all | solution.py:93
  22.6 7.0 %copy-start.2 = (bf16[1,16,256,1280]{3,2,1,0:T(8,128)(2,1)S(1)}, bf16[1,16,256,1280]{3,2,1,0:T(8,128)(2,1)}, u32[]{:S(2)}) copy-start(bf16[1,16,256,1280]{3,2,1,0:T(8,128)(2,1)} %param.6) | copy-start | bytes 31457284
  39.5 21.5 %all-to-all-start = ((bf16[16,1,128,240]{2,3,1,0:T(8,128)(2,1)}), bf16[16,1,128,240]{2,3,1,0:T(8,128)(2,1)S(1)}, u32[]{:S(2)}, u32[]{:S(2)}) async-start(bf16[16,1,128,240]{2,3,1,0:T(8,128)(2,1)} %copy.18), calls=%async_computation | async-start | bytes 1966080 | tf_op jit(solution)/shard_map/all_to_all | solution.py:88
  45.2 232.2 %reduce-scatter.2.cloned.1.call-start = ((), (), s32[]{:S(2)}) async-start(), calls=%async_computation.4 | async-start | bytes 20889600 | tf_op jit(solution)/shard_map/reduce_scatter | solution.py:100
  164.9 207.2 %copy-start.1 = (bf16[1280,8]{0,1:T(8,128)(2,1)S(1)}, bf16[1280,8]{0,1:T(8,128)(2,1)}, u32[]{:S(2)}) copy-start(bf16[1280,8]{0,1:T(8,128)(2,1)} %param.7) | copy-start | bytes 61444
  164.9 204.8 %all-reduce.2.cloned.1.call-start = ((), (), s32[]{:S(2)}) async-start(), calls=%async_computation.5 | async-start | bytes 2457600 | tf_op jit(solution)/shard_map/psum | solution.py:101
Sparse Core Ops, SparseCore 0:
  165.0 112.3 reduce-scatter.1
  280.1 89.5 all-reduce.1
